TPU v7x, 32 devices: a whole 2x2x4 slice. The times are simulated.
32 devices in a mesh: bond: 8 (over y, x, core), mpo: 4 (over z).
Axes of the slice: x: 2, y: 2, z: 4, core: 2. Of those that a mesh axis runs over, the one named last changes fastest.
Arguments:
- carried: bfloat16 [198, 8192], P(None, 'bond'), may hold values from -6 to 6
- site_tensors: bfloat16 [2, 8192, 4, 8192], P(None, 'bond', 'mpo'), may hold values from -0.09375 to 0.09375
- operator_tensors: bfloat16 [2, 4, 66, 264], replicated, may hold values from -0.375 to 0.375
- rotation: bfloat16 [2, 8192, 4, 8192], P(None, 'bond', 'mpo'), may hold values from -0.09375 to 0.09375
- kept_columns: int32 [2, 8192], replicated, may hold values from 0 to 32767, as said below
Outputs:
- rotated_state: bfloat16 [198, 8192], P(None, 'bond')
- truncation_gram: float32 [2, 198, 198], replicated
Inputs may be any that keep to these rules, and one draw needn't show every extreme that they name: `kept_columns`: each row holds 8192 distinct values; value r * 4 + t names right-bond index r and physical index t.
All inputs are finite; a program needn't handle non-finite values.
Results may differ from a plain program's by a relative error of at most 0.035.
Values may be sent and summed in bfloat16 or wider, within the bound.
A program may use at most 128 MiB of HBM per device.

v0:
```python
import jax
import jax.numpy as jnp
from jax import lax
from jax.sharding import PartitionSpec as P

BOND_DIM = 8192
PHYSICAL = 4
MPO_BOND = 66
LEFT_ROWS = 3
SITE_COUNT = 2


def on_device(carried, site_tensors, operator_tensors, rotation, kept_columns):
    row_count = carried.shape[0]
    bond_block = carried.shape[1]
    phys_local = site_tensors.shape[2]
    state = carried
    gram_list = []
    for position in range(SITE_COUNT):
        tensor = site_tensors[position].reshape(bond_block, phys_local * BOND_DIM)
        partial_sum = jnp.dot(state, tensor, preferred_element_type=jnp.float32)
        partial_sum = partial_sum.reshape(row_count, phys_local, BOND_DIM)
        summed = lax.psum_scatter(
            partial_sum.astype(jnp.bfloat16), "bond", scatter_dimension=2, tiled=True
        )
        contracted = summed.reshape(LEFT_ROWS, MPO_BOND, phys_local, bond_block)
        weights = lax.dynamic_slice_in_dim(
            operator_tensors[position], lax.axis_index("mpo") * phys_local, phys_local, 0
        )
        mixed_rows = jnp.einsum(
            "lasr,sac->lcr", contracted, weights, preferred_element_type=jnp.float32
        )
        mixed_rows = mixed_rows.reshape(LEFT_ROWS, PHYSICAL, MPO_BOND, bond_block)
        mixed_rows = lax.psum_scatter(
            mixed_rows.astype(jnp.bfloat16), "mpo", scatter_dimension=1, tiled=True
        ).astype(jnp.float32)
        out_local = mixed_rows.shape[1]
        chosen = jnp.zeros((PHYSICAL * BOND_DIM,), jnp.float32).at[kept_columns[position]].set(1.0)
        chosen = chosen.reshape(BOND_DIM, PHYSICAL)
        chosen = lax.dynamic_slice(
            chosen,
            (lax.axis_index("bond") * bond_block, lax.axis_index("mpo") * out_local),
            (bond_block, out_local),
        )
        kept_rows = (mixed_rows * chosen.T[None, :, None, :]).astype(jnp.bfloat16)
        gram_matrix = jnp.einsum(
            "ltar,mtbr->lamb", kept_rows, kept_rows, preferred_element_type=jnp.float32
        )
        gram_matrix = gram_matrix.reshape(row_count, row_count) / BOND_DIM
        gram_list.append(lax.psum(gram_matrix, ("bond", "mpo")))
        rotated = jnp.einsum(
            "ltbr,rtq->lbq", kept_rows, rotation[position], preferred_element_type=jnp.float32
        )
        rotated = rotated.reshape(row_count, BOND_DIM)
        rotated_part = lax.psum_scatter(
            rotated.astype(jnp.bfloat16), "bond", scatter_dimension=1, tiled=True
        ).astype(jnp.float32)
        rotated_part = lax.psum(rotated_part.astype(jnp.bfloat16), "mpo").astype(jnp.float32)
        state = rotated_part.astype(jnp.bfloat16)
    return (state, jnp.stack(gram_list))


def solution(mesh):
    return jax.shard_map(
        on_device,
        mesh=mesh,
        in_specs=(
            P(None, "bond"),
            P(None, "bond", "mpo", None),
            P(),
            P(None, "bond", "mpo", None),
            P(),
        ),
        out_specs=(P(None, "bond"), P()),
        check_vma=False,
    )
```

profile of v0, /device:TPU:0, one launch (start us, length us, event | category | flops | bytes accessed | tf_op | source)
XLA Modules:
  0.0 624.9 jit_solution(11035571024467645887)
XLA Ops:
  7.2 0.9 copy-done
  8.2 11.0 %fusion.27 = bf16[198,1,8192]{2,0,1:T(8,128)(2,1)} fusion(bf16[198,1024]{1,0:T(8,128)(2,1)S(1)} %copy-done, bf16[2,1024,1,8192]{3,1,2,0:T(8,128)(2,1)} %param.6), kind=kOutput, calls=%fused_computation.19 | convolution fusion | flops 3323510784 | bytes 20426752 | tf_op jit(solution)/shard_map/dot_general | solution.py:21
  19.2 0.0 all-reduce.13.cloned.1.call-start
  19.3 0.1 fusion.38
  19.5 0.1 constant_dynamic-slice_fusion
  19.6 49.4 %reduce-scatter.7.cloned.1.call-done = bf16[198,1,1024]{2,0,1:T(8,128)(2,1)} async-done(((bf16[198,1,8192]{2,0,1:T(8,128)(2,1)}), bf16[198,1,1024]{2,0,1:T(8,128)(2,1)}) %reduce-scatter.7.cloned.1.call-update) | async-done | bytes 405520 | tf_op jit(solution)/shard_map/reduce_scatter | solution.py:23
  69.0 1.1 reshape.132
  70.1 0.6 fusion.30
  70.7 2.0 convert_element_type.60
  72.7 0.0 reduce-scatter.9.cloned.1.call-start
  72.7 0.1 compare_select_fusion
  72.8 30.5 %scatter_custom_fusion = f32[32768]{0:T(1024)S(1)} fusion(s32[8192]{0:T(1024)S(1)} %bitcast.74, f32[8192]{0:T(1024)S(1)} %broadcast.52, f32[]{:T(128)} %constant.9.clone.1), kind=kCustom, calls=%fused_computation.37 | custom fusion | bytes 131076 | tf_op jit(solution)/shard_map/scatter | solution.py:38
  103.4 5.6 reshape.133
  109.0 0.6 dynamic-slice.2
  109.6 1.4 dynamic-slice_reduce_fusion.1
  111.0 37.4 %all-reduce.13.cloned.1.call-done = bf16[3,4,66,1024]{3,2,1,0:T(8,128)(2,1)} async-done(((bf16[3,4,66,1024]{3,2,1,0:T(8,128)(2,1)}), bf16[3,4,66,1024]{3,2,1,0:T(8,128)(2,1)}) %all-reduce.13.cloned.1.call-update) | async-done | bytes 1622032
  148.4 1.8 multiply_convert_fusion.1
  150.1 0.1 dot_general.30
  150.2 11.0 %fusion.15 = bf16[198,8192]{1,0:T(8,128)(2,1)} fusion(bf16[198,1024]{1,0:T(8,128)(2,1)S(1)} %dot_general.30, bf16[2,1024,1,8192]{3,1,2,0:T(8,128)(2,1)} %param.8), kind=kOutput, calls=%fused_computation.15 | convolution fusion | flops 3323510784 | bytes 20426752 | tf_op jit(solution)/shard_map/ltbr,rtq->lbq/dot_general | solution.py:51
  161.3 0.0 all-reduce.9.cloned.1.call-start
  161.3 46.1 %reduce-scatter.9.cloned.1.call-done = bf16[198,1024]{1,0:T(8,128)(2,1)} async-done(((bf16[198,8192]{1,0:T(8,128)(2,1)}), bf16[198,1024]{1,0:T(8,128)(2,1)}) %reduce-scatter.9.cloned.1.call-update) | async-done | bytes 405520 | tf_op jit(solution)/shard_map/reduce_scatter | solution.py:55
  207.4 0.2 reduce-scatter.11.cloned.1.call-start
  207.6 39.0 %all-reduce.9.cloned.1.call-done = bf16[198,1024]{1,0:T(8,128)(2,1)} async-done(((bf16[198,1024]{1,0:T(8,128)(2,1)}), bf16[198,1024]{1,0:T(8,128)(2,1)}) %all-reduce.9.cloned.1.call-update) | async-done | bytes 405520 | tf_op jit(solution)/shard_map/psum | solution.py:58
  246.7 11.2 %fusion.24 = bf16[198,1,8192]{2,0,1:T(8,128)(2,1)} fusion(bf16[198,1024]{1,0:T(8,128)(2,1)} %all-reduce.9.cloned.1.call-done, bf16[2,1024,1,8192]{3,1,2,0:T(8,128)(2,1)} %param.6), kind=kOutput, calls=%fused_computation.18 | convolution fusion | flops 3323510784 | bytes 20430848 | tf_op jit(solution)/shard_map/dot_general | solution.py:21
  257.9 0.0 all-reduce.15.cloned.1.call-start
  257.9 0.1 constant_dynamic-slice_fusion.1
  258.0 46.6 %reduce-scatter.11.cloned.1.call-done = bf16[198,1,1024]{2,0,1:T(8,128)(2,1)} async-done(((bf16[198,1,8192]{2,0,1:T(8,128)(2,1)}), bf16[198,1,1024]{2,0,1:T(8,128)(2,1)}) %reduce-scatter.11.cloned.1.call-update) | async-done | bytes 405520 | tf_op jit(solution)/shard_map/reduce_scatter | solution.py:23
  304.7 1.1 reshape.135
  305.8 0.6 fusion.31
  306.4 2.0 convert_element_type.68
  308.4 0.0 reduce-scatter.13.cloned.1.call-start
  308.4 30.5 %scatter_custom_fusion.1 = f32[32768]{0:T(1024)S(1)} fusion(s32[8192]{0:T(1024)S(1)} %bitcast.73, f32[8192]{0:T(1024)S(1)} %broadcast.52, f32[]{:T(128)} %constant.9.clone.1), kind=kCustom, calls=%fused_computation.35 | custom fusion | bytes 131076 | tf_op jit(solution)/shard_map/scatter | solution.py:38
  338.9 5.6 reshape.136
  344.6 1.4 dynamic-slice_reduce_fusion
  346.0 38.0 %all-reduce.15.cloned.1.call-done = bf16[3,4,66,1024]{3,2,1,0:T(8,128)(2,1)} async-done(((bf16[3,4,66,1024]{3,2,1,0:T(8,128)(2,1)}), bf16[3,4,66,1024]{3,2,1,0:T(8,128)(2,1)}) %all-reduce.15.cloned.1.call-update) | async-done | bytes 1622032
  384.0 1.7 multiply_convert_fusion
  385.8 0.1 dot_general.34
  385.9 11.0 %fusion.21 = bf16[198,8192]{1,0:T(8,128)(2,1)} fusion(bf16[198,1024]{1,0:T(8,128)(2,1)S(1)} %dot_general.34, bf16[2,1024,1,8192]{3,1,2,0:T(8,128)(2,1)} %param.8), kind=kOutput, calls=%fused_computation.17 | convolution fusion | flops 3323510784 | bytes 20426752 | tf_op jit(solution)/shard_map/ltbr,rtq->lbq/dot_general | solution.py:51
  396.9 0.0 all-reduce.17.cloned.1.call-start
  397.0 1.0 fusion.33
  398.0 1.0 fusion.32
  399.0 0.0 all-reduce.11.cloned.1.call-start
  399.0 44.0 %reduce-scatter.13.cloned.1.call-done = bf16[198,1024]{1,0:T(8,128)(2,1)} async-done(((bf16[198,8192]{1,0:T(8,128)(2,1)}), bf16[198,1024]{1,0:T(8,128)(2,1)}) %reduce-scatter.13.cloned.1.call-update) | async-done | bytes 405520 | tf_op jit(solution)/shard_map/reduce_scatter | solution.py:55
  443.1 133.2 %all-reduce.17.cloned.1.call-done = (f32[1,198,198]{2,1,0:T(8,128)}, f32[1,198,198]{2,1,0:T(8,128)}) async-done(((f32[1,198,198]{2,1,0:T(8,128)}, f32[1,198,198]{2,1,0:T(8,128)}), (f32[1,198,198]{2,1,0:T(8,128)}, f32[1,198,198]{2,1,0:T(8,128)})) %all-reduce.17.cloned.1.call-update) | async-done | bytes 313648 | tf_op jit(solution)/shard_map/psum | solution.py:50
  576.3 1.1 pad_maximum_fusion
  577.3 1.0 copy.13
  578.3 38.2 %all-reduce.11.cloned.1.call-done = bf16[198,1024]{1,0:T(8,128)(2,1)} async-done(((bf16[198,1024]{1,0:T(8,128)(2,1)}), bf16[198,1024]{1,0:T(8,128)(2,1)}) %all-reduce.11.cloned.1.call-update) | async-done | bytes 405520 | tf_op jit(solution)/shard_map/psum | solution.py:58
  616.5 1.8 copy.32
  (20 shorter events, 0.2 us)
Async XLA Ops:
  7.2 1.0 copy-start
  7.2 12.1 %copy-start.2 = (bf16[2,4,66,264]{3,1,2,0:T(4,128)(2,1)S(1)}, bf16[2,4,66,264]{3,1,2,0:T(4,128)(2,1)}, u32[]{:S(2)}) copy-start(bf16[2,4,66,264]{3,1,2,0:T(4,128)(2,1)} %param.7) | copy-start | bytes 836356
  7.2 61.8 %reduce-scatter.7.cloned.1.call-start = ((), (), s32[]{:S(2)}) async-start(), calls=%async_computation.4 | async-start | bytes 3686400 | tf_op jit(solution)/shard_map/reduce_scatter | solution.py:23
  19.2 129.1 %all-reduce.13.cloned.1.call-start = ((), (), s32[]{:S(2)}) async-start(), calls=%async_computation.10 | async-start | bytes 3538944
  19.4 53.3 %copy-start.3 = (s32[2,8192]{1,0:T(2,128)S(1)}, s32[2,8192]{1,0:T(2,128)}, u32[]{:S(2)}) copy-start(s32[2,8192]{1,0:T(2,128)} %param.9) | copy-start | bytes 196612
  70.7 38.3 %copy-start.4 = (u32[32]{0:T(128)S(1)}, u32[32]{0:T(128)}, u32[]{:S(2)}) copy-start(u32[32]{0:T(128)} %constant.34) | copy-start | bytes 388
  72.7 134.7 %reduce-scatter.9.cloned.1.call-start = ((), (), s32[]{:S(2)}) async-start(), calls=%async_computation.5 | async-start | bytes 3686400 | tf_op jit(solution)/shard_map/reduce_scatter | solution.py:55
  161.3 85.4 %all-reduce.9.cloned.1.call-start = ((), (), s32[]{:S(2)}) async-start(), calls=%async_computation.6 | async-start | bytes 819200 | tf_op jit(solution)/shard_map/psum | solution.py:58
  207.4 97.3 %reduce-scatter.11.cloned.1.call-start = ((), (), s32[]{:S(2)}) async-start(), calls=%async_computation.7 | async-start | bytes 3686400 | tf_op jit(solution)/shard_map/reduce_scatter | solution.py:23
  257.9 126.2 %all-reduce.15.cloned.1.call-start = ((), (), s32[]{:S(2)}) async-start(), calls=%async_computation.11 | async-start | bytes 3538944
  308.4 134.7 %reduce-scatter.13.cloned.1.call-start = ((), (), s32[]{:S(2)}) async-start(), calls=%async_computation.8 | async-start | bytes 3686400 | tf_op jit(solution)/shard_map/reduce_scatter | solution.py:55
  396.9 221.4 %copy-start.1 = (bf16[198,1024]{1,0:T(8,128)(2,1)S(1)}, bf16[198,1024]{1,0:T(8,128)(2,1)}, u32[]{:S(2)}) copy-start(bf16[198,1024]{1,0:T(8,128)(2,1)} %param.5) | copy-start | bytes 1216516
  396.9 179.3 %all-reduce.17.cloned.1.call-start = ((), (), s32[]{:S(2)}) async-start(), calls=%async_computation.12 | async-start | bytes 819200 | tf_op jit(solution)/shard_map/psum | solution.py:50
  399.0 217.6 %all-reduce.11.cloned.1.call-start = ((), (), s32[]{:S(2)}) async-start(), calls=%async_computation.9 | async-start | bytes 819200 | tf_op jit(solution)/shard_map/psum | solution.py:58
Sparse Core Ops, SparseCore 0:
  19.3 49.5 reduce-scatter.6
  72.8 75.5 all-reduce.12
  161.4 45.9 reduce-scatter.8
  209.7 36.9 all-reduce.8
  258.0 46.6 reduce-scatter.10
  308.5 75.4 all-reduce.14
  397.1 45.9 reduce-scatter.12
  449.9 126.3 all-reduce.16
  578.6 37.8 all-reduce.10
where the time goes:
time: 625 us
  waiting for transfers between devices  472 us (76%)
  local copies, waits for them, and re-layouts  86.1 us (14%)
  matrix products  47.4 us (8%)
  between operations  14 us (2%)
    psum x1, waiting for transfers between devices, on_device(): gram_list.append(lax.psum(gram_matrix, ('bond', 'mpo')))  133 us
    reduce_scatter x2, waiting for transfers between devices, on_device(): lax.psum_scatter(partial_sum.astype(jnp.bfloat16), 'bond', scatter_dimens...  96 us
    reduce_scatter x2, waiting for transfers between devices, on_device(): lax.psum_scatter(rotated.astype(jnp.bfloat16), 'bond', scatter_dimension=...  90.1 us
    psum x2, waiting for transfers between devices, on_device(): lax.psum(rotated_part.astype(jnp.bfloat16), 'mpo').astype(jnp.float32)  77.3 us
    unnamed x11, waiting for transfers between devices  75.6 us
    scatter x2, local copies, waits for them, and re-layouts, on_device(): jnp.zeros((PHYSICAL * BOND_DIM,), jnp.float32).at[kept_columns[position]]  61 us
    dot_general x2, matrix products, on_device(): partial_sum = jnp.dot(state, tensor, preferred_element_type=jnp.float32)  22.2 us
    dot_general x2, matrix products, on_device(): jnp.einsum('ltbr,rtq->lbq', kept_rows, rotation[position], preferred_elem...  22 us
  transfers between devices with their start and end apart: 9, of which 9 were waited for; matrix products, arithmetic and copies ran while one was open for 13% of the time, Pallas kernels for 0%

commit v1 on v0

v1 whole, which is shorter than its diff:
```python
import functools

import jax
import jax.numpy as jnp
from jax import lax
from jax.experimental import pallas as pl
from jax.experimental.pallas import tpu as pltpu
from jax.sharding import PartitionSpec as P

LEFT_ROWS = 3
SITE_COUNT = 2
MESH = pl.DeviceIdType.MESH
F32 = jnp.float32
BF16 = jnp.bfloat16


def flip(index, bit):
    return index + (1 - 2 * ((index // (1 << bit)) % 2)) * (1 << bit)


def xor_bits(index, other, bits):
    out = 0
    for b in range(bits):
        out = out + (((index // (1 << b)) % 2 + (other // (1 << b)) % 2) % 2) * (1 << b)
    return out


def reverse_bits(index, bits):
    out = 0
    for b in range(bits):
        out = out + ((index // (1 << b)) % 2) * (1 << (bits - 1 - b))
    return out


def z_roles():
    z = lax.axis_index("mpo")
    is_mid = (z == 1) | (z == 2)
    inner = jnp.where(z == 0, 1, 2)
    outer = jnp.where(z == 1, 0, 3)
    return z, is_mid, inner, outer, 3 - z


def site_kernel(bits, chunks, site, mixing, *refs):
    if mixing:
        (state, weight, ops, mask, out, gram,
         wbuf, psend, own, prec, xrec, cg, zsend, zrec,
         wsem, pss, prs, xss, xrs, zss, zrs) = refs
    else:
        (state, weight, out,
         wbuf, psend, own, prec, xrec, zown, zin, zsum, zrec,
         wsem, pss, prs, xss, xrs, zss, zrs) = refs
    chips = 1 << bits
    depth = state.shape[1]
    rows = state.shape[0]
    block = weight.shape[2] // (2 * chips)
    width = block // chunks
    half = width // 2
    j = lax.axis_index("bond")
    me, core = j // 2, j % 2
    z, is_mid, inner, outer, across = z_roles()
    is_end = jnp.logical_not(is_mid)

    def weight_copy(c, other, r):
        dest = 2 * xor_bits(me, r, bits) + (1 - core if other else core)
        start = pl.multiple_of(dest * block + c * width, 128)
        slot = (c * 2 + (0 if other else 1)) * chips + r
        return pltpu.make_async_copy(
            weight.at[site, :, pl.ds(start, width)], wbuf.at[slot], wsem.at[slot]
        )

    for c in range(chunks):
        for other in (True, False):
            @pl.loop(0, chips)
            def _(r):
                weight_copy(c, other, r).start()

    barrier = pltpu.get_barrier_semaphore()

    def greet(bond, mpo):
        pl.semaphore_signal(barrier, inc=1, device_id=(bond, mpo), device_id_type=MESH)

    greet(2 * me + 1 - core, z)
    for b in range(bits):
        greet(2 * flip(me, b) + core, z)

    @pl.when(is_mid)
    def _():
        greet(j, outer)
        greet(j, across)
        pl.semaphore_wait(barrier, bits + 3)

    @pl.when(is_end)
    def _():
        greet(j, inner)
        pl.semaphore_wait(barrier, bits + 2)

    def remote(src, dst, ss, rs, bond, mpo):
        return pltpu.make_async_remote_copy(
            src_ref=src, dst_ref=dst, send_sem=ss, recv_sem=rs,
            device_id=(bond, mpo), device_id_type=MESH,
        )

    def pair_copy(c):
        return remote(psend.at[c], prec.at[c], pss.at[c], prs.at[c], 2 * me + 1 - core, z)

    def xy_copy(c, step, side):
        n = chips >> (step + 1)
        bit = bits - 1 - step if side == 0 else step
        return remote(
            own.at[c, side, pl.ds(n, n)], xrec.at[c, side, pl.ds(n, n)],
            xss.at[c, step, side], xrs.at[c, step, side], 2 * flip(me, bit) + core, z,
        )

    def multiply(c):
        for other, target in ((True, psend), (False, own)):
            @pl.loop(0, chips)
            def _(r):
                weight_copy(c, other, r).wait()
                slot = (c * 2 + (0 if other else 1)) * chips + r
                product = jnp.dot(state[...], wbuf[slot], preferred_element_type=F32).astype(BF16)
                target[c, 0, r] = product[:, :half]
                target[c, 1, reverse_bits(r, bits)] = product[:, half:]

            if other:
                pair_copy(c).start()

    def pair_sum(c):
        pair_copy(c).wait_recv()
        for side in range(2):
            own[c, side] = (own[c, side].astype(F32) + prec[c, side].astype(F32)).astype(BF16)
            xy_copy(c, 0, side).start()

    def xy_sum(c, step):
        n = chips >> (step + 1)
        parts = []
        for side in range(2):
            xy_copy(c, step, side).wait_recv()
            total = (own[c, side, pl.ds(0, n)].astype(F32)
                     + xrec[c, side, pl.ds(n, n)].astype(F32)).astype(BF16)
            if step < bits - 1:
                own[c, side, pl.ds(0, n)] = total
                xy_copy(c, step + 1, side).start()
            else:
                parts.append(total[0])
        return parts

    columns = [pl.ds(c * width, width) for c in range(chunks)]

    if mixing:
        def z_end_copy(c, slot):
            return remote(cg.at[c, slot], cg.at[c, slot],
                          zss.at[c, 0], zrs.at[c, 0], j, jnp.where(is_mid, outer, inner))

        def z_own_copy(c, slot):
            return remote(cg.at[c, slot], cg.at[c, slot],
                          zss.at[c, 1], zrs.at[c, 1], j, jnp.where(is_mid, across, inner))

        def z_pass_copy(c, slot):
            return remote(cg.at[c, slot], cg.at[c, slot],
                          zss.at[c, 2], zrs.at[c, 2], j, jnp.where(is_mid, across, inner))

        def z_back_copy(c):
            return remote(zsend.at[c], zrec.at[c],
                          zss.at[c, 3], zrs.at[c, 3], j, jnp.where(is_mid, outer, inner))

        def z_first(c, parts):
            cg[c, z, :, pl.ds(0, half)] = parts[0]
            cg[c, z, :, pl.ds(half, half)] = parts[1]

            @pl.when(is_end)
            def _():
                z_end_copy(c, z).start()

            @pl.when(is_mid)
            def _():
                z_own_copy(c, z).start()

        def z_second(c):
            @pl.when(is_mid)
            def _():
                z_end_copy(c, outer).wait_recv()
                z_pass_copy(c, outer).start()

        def mix(c, which):
            total = jnp.dot(ops[site, which, 0], cg[c, 0], preferred_element_type=F32)
            for s in range(1, 4):
                total += jnp.dot(ops[site, which, s], cg[c, s], preferred_element_type=F32)
            return total

        def keep(c, mixed):
            kept = (mixed * mask[:, columns[c]]).astype(BF16)
            out[:, columns[c]] = kept
            square = lax.dot_general(kept, kept, (((1,), (1,)), ((), ())),
                                     preferred_element_type=F32)
            if c == 0:
                gram[...] = square
            else:
                gram[...] += square

        def z_third(c):
            @pl.when(is_mid)
            def _():
                z_own_copy(c, across).wait_recv()
                z_pass_copy(c, 3 - outer).wait_recv()
                zsend[c] = mix(c, 1).astype(BF16)
                z_back_copy(c).start()
                keep(c, mix(c, 0))

        def z_fourth(c):
            @pl.when(is_end)
            def _():
                z_back_copy(c).wait_recv()
                keep(c, zrec[c].astype(F32))

        end_sends = (lambda c: z_end_copy(c, z),)
        mid_sends = (lambda c: z_own_copy(c, z), lambda c: z_pass_copy(c, outer), z_back_copy)
    else:
        def z_end_copy(c):
            return remote(zown.at[c], zin.at[c],
                          zss.at[c, 0], zrs.at[c, 0], j, jnp.where(is_mid, outer, inner))

        def z_mid_copy(c):
            return remote(zsum.at[c], zrec.at[c],
                          zss.at[c, 1], zrs.at[c, 1], j, jnp.where(is_mid, across, inner))

        def z_back_copy(c):
            return remote(zown.at[c], zin.at[c],
                          zss.at[c, 2], zrs.at[c, 2], j, jnp.where(is_mid, outer, inner))

        def z_first(c, parts):
            zown[c, :, pl.ds(0, half)] = parts[0]
            zown[c, :, pl.ds(half, half)] = parts[1]

            @pl.when(is_end)
            def _():
                z_end_copy(c).start()

        def z_second(c):
            @pl.when(is_mid)
            def _():
                z_end_copy(c).wait_recv()
                zsum[c] = (zown[c].astype(F32) + zin[c].astype(F32)).astype(BF16)
                z_mid_copy(c).start()

        def z_third(c):
            @pl.when(is_mid)
            def _():
                z_mid_copy(c).wait_recv()
                total = (zsum[c].astype(F32) + zrec[c].astype(F32)).astype(BF16)
                zown[c] = total
                z_back_copy(c).start()
                out[:, columns[c]] = total

        def z_fourth(c):
            @pl.when(is_end)
            def _():
                z_back_copy(c).wait_recv()
                out[:, columns[c]] = zin[c]

        end_sends, mid_sends = (z_end_copy,), (z_mid_copy, z_back_copy)

    stages = [multiply, pair_sum]
    for step in range(bits - 1):
        stages.append(functools.partial(xy_sum, step=step))
    stages += [lambda c: z_first(c, xy_sum(c, bits - 1)), z_second, z_third, z_fourth]
    for t in range(chunks + len(stages) - 1):
        for number, stage in enumerate(stages):
            if 0 <= t - number < chunks:
                stage(t - number)

    for c in range(chunks):
        pair_copy(c).wait_send()
        for step in range(bits):
            for side in range(2):
                xy_copy(c, step, side).wait_send()

        @pl.when(is_end)
        def _():
            for copy in end_sends:
                copy(c).wait_send()

        @pl.when(is_mid)
        def _():
            for copy in mid_sends:
                copy(c).wait_send()


def apply_site(bits, site, mixing, state, weight, *extra):
    rows, depth = state.shape
    chips = 1 << bits
    block = weight.shape[2] // (2 * chips)
    chunks = max(1, block // 256)
    width = block // chunks
    half = width // 2
    vmem = pl.BlockSpec(memory_space=pltpu.VMEM)
    parts = pltpu.VMEM((chunks, 2, chips, rows, half), BF16)
    piece = pltpu.VMEM((chunks, rows, width), BF16)
    out_shape = [jax.ShapeDtypeStruct((rows, block), BF16)]
    if mixing:
        out_shape.append(jax.ShapeDtypeStruct((rows, rows), F32))
        z_scratch = [pltpu.VMEM((chunks, 4, rows, width), BF16), piece, piece]
    else:
        z_scratch = [piece] * 4
    dma = pltpu.SemaphoreType.DMA
    z_copies = 4 if mixing else 3
    return pl.pallas_call(
        functools.partial(site_kernel, bits, chunks, site, mixing),
        out_shape=out_shape,
        in_specs=[vmem, pl.BlockSpec(memory_space=pl.ANY)] + [vmem] * len(extra),
        out_specs=[vmem] * len(out_shape),
        scratch_shapes=[
            pltpu.VMEM((2 * chips * chunks, depth, width), BF16),
            parts, parts, parts, parts,
            *z_scratch,
            dma((2 * chips * chunks,)),
            dma((chunks,)), dma((chunks,)),
            dma((chunks, bits, 2)), dma((chunks, bits, 2)),
            dma((chunks, z_copies)), dma((chunks, z_copies)),
        ],
        compiler_params=pltpu.CompilerParams(
            collective_id=2 * site + (0 if mixing else 1),
            has_side_effects=True,
            vmem_limit_bytes=48 * 1024 * 1024,
        ),
        cost_estimate=pl.CostEstimate(
            flops=2 * rows * depth * weight.shape[2],
            bytes_accessed=2 * depth * weight.shape[2],
            transcendentals=0,
        ),
    )(state, weight, *extra)


def operator_blocks(operator_tensors, rows):
    bonds = operator_tensors.shape[2]
    z, is_mid, inner, outer, across = z_roles()
    found = []
    for t in (z, jnp.where(is_mid, outer, inner)):
        found.append(lax.dynamic_slice_in_dim(operator_tensors, t * bonds, bonds, 3))
    ops = jnp.stack(found, axis=1).swapaxes(3, 4)
    keep = ((0, 0),) * 3
    blocks = []
    for l in range(LEFT_ROWS):
        place = (l * bonds, rows - (l + 1) * bonds)
        blocks.append(jnp.pad(ops, keep + (place, place)))
    return functools.reduce(jnp.add, blocks)


def chosen_columns(kept_columns, physical, block):
    index = kept_columns // physical - lax.axis_index("bond") * block
    mine = (kept_columns % physical) == lax.axis_index("mpo")
    high = jnp.where(mine & (index >= 0), index // 128, -1)
    low = index % 128
    high = (high[:, :, None] == jnp.arange(block // 128)).astype(BF16)
    low = (low[:, :, None] == jnp.arange(128)).astype(BF16)
    marks = jnp.einsum("khi,khj->kij", high, low, preferred_element_type=F32)
    return marks.reshape(kept_columns.shape[0], 1, block)


def solution(mesh):
    bits = (mesh.shape["bond"] // 2).bit_length() - 1

    def on_device(carried, site_tensors, operator_tensors, rotation, kept_columns):
        row_count, block = carried.shape
        rows = -(-row_count // 16) * 16
        physical = operator_tensors.shape[1]
        sites = site_tensors.reshape(site_tensors.shape[0], block, -1)
        turns = rotation.reshape(rotation.shape[0], block, -1)
        ops = operator_blocks(operator_tensors, rows)
        mask = chosen_columns(kept_columns, physical, block)
        state = jnp.pad(carried, ((0, rows - row_count), (0, 0)))
        grams = []
        for site in range(SITE_COUNT):
            kept, gram = apply_site(bits, site, True, state, sites, ops, mask[site])
            gram = gram[:row_count, :row_count] / (block * mesh.shape["bond"])
            grams.append(lax.psum(gram, ("bond", "mpo")))
            (state,) = apply_site(bits, site, False, kept, turns)
        return state[:row_count], jnp.stack(grams)

    return jax.shard_map(
        on_device,
        mesh=mesh,
        in_specs=(
            P(None, "bond"),
            P(None, "bond", "mpo", None),
            P(),
            P(None, "bond", "mpo", None),
            P(),
        ),
        out_specs=(P(None, "bond"), P()),
        check_vma=False,
    )
```

time: 625 us -> 269 us (0.43)
  waiting for transfers between devices: 472 us -> 87.4 us
  Pallas kernels: 0 us -> 158 us
  local copies, waits for them, and re-layouts: 86.1 us -> 2.38 us
  matrix products: 47.4 us -> 2.55 us
    reduce_scatter x4 -> x0, waiting for transfers between devices: 186 us -> none  [the longest x2 96 us: on_device(): lax.psum_scatter(partial_sum.astype(jnp.bfloat16), 'bond', scatter_dimens...]
    pallas_call x0 -> x4, Pallas kernels: none -> 158 us  [apply_site(): pl.pallas_call(functools.partial(site_kernel, bits, chunks, site, mixing)...]
    psum x3 -> x1, waiting for transfers between devices: 210 us -> 87.4 us  [on_device(): grams.append(lax.psum(gram, ('bond', 'mpo')))]
    unnamed x11 -> x1, waiting for transfers between devices: 75.6 us -> 0.02 us
    scatter x2 -> x0, local copies, waits for them, and re-layouts: 61 us -> none  [on_device(): jnp.zeros((PHYSICAL * BOND_DIM,), jnp.float32).at[kept_columns[position]]]
    dot_general x8 -> x1, matrix products: 47.4 us -> 2.55 us  [chosen_columns(): marks = jnp.einsum('khi,khj->kij', high, low, preferred_element_type=F32)]
    reshape x2 -> x0, local copies, waits for them, and re-layouts: 11.3 us -> none  [on_device(): chosen = chosen.reshape(BOND_DIM, PHYSICAL)]
  transfers between devices with their start and end apart: 9 -> 1, of which waited for: 9 -> 1; matrix products, arithmetic and copies ran while one was open for 13% -> 0% of each run, Pallas kernels for 0% -> 14%
where the time goes in v1:
time: 269 us
  Pallas kernels  158 us (59%)
  waiting for transfers between devices  87.4 us (32%)
  between operations  14.1 us (5%)
  other arithmetic  3.8 us (1%)
    pallas_call x4, Pallas kernels, apply_site(): pl.pallas_call(functools.partial(site_kernel, bits, chunks, site, mixing)...  158 us
    psum x1, waiting for transfers between devices, on_device(): grams.append(lax.psum(gram, ('bond', 'mpo')))  87.4 us
  transfers between devices with their start and end apart: 1, of which 1 were waited for; matrix products, arithmetic and copies ran while one was open for 0% of the time, Pallas kernels for 14%

profile of v1, /device:TPU:0, one launch (start us, length us, event | category | flops | bytes accessed | tf_op | source)
XLA Modules:
  0.0 268.8 jit_solution(787003537636454683)
XLA Ops:
  7.2 0.0 copy-start.1
  7.2 0.0 all-reduce.7.cloned.1.call-start
  7.2 1.3 and_select_fusion.2
  8.5 0.1 and_select_fusion
  8.6 0.0 copy-start
  8.6 2.5 fusion
  11.2 0.0 copy-done.1
  11.2 0.2 constant_dynamic-slice_fusion.1
  11.4 0.2 copy.7
  11.6 0.2 copy.8
  11.8 0.1 maximum_bitcast_fusion
  11.9 0.5 pad_add_fusion.refs_2_
  12.4 0.0 copy-done
  12.5 43.7 %shard_map.68 = (bf16[208,1024]{1,0:T(8,128)(2,1)S(1)}, f32[208,208]{1,0:T(8,128)S(1)}) custom-call(bf16[208,1024]{1,0:T(8,128)(2,1)S(1)} %pad.16.refs_0_, bf16[2,1024,8192]{2,1,0:T(8,128)(2,1)} %bitcast.14, bf16[2,2,4,208,208]{4,3,2,1,0:T(8,128)(2,1)S(1)} %pad_add_fusion.refs_2_, f32[1,1024]{1,0:T(1,128)S(1)} %bitcast.13), custom_call_target="tpu_custom_call" | custom-call | flops 3489660928 | bytes 16777216 | tf_op jit(solution)/shard_map/pallas_call | solution.py:306
  56.2 36.7 %shard_map.69.refs_0_ = bf16[208,1024]{1,0:T(8,128)(2,1)S(1)} custom-call(bf16[208,1024]{1,0:T(8,128)(2,1)S(1)} %get-tuple-element.6.refs_0_, bf16[2,1024,8192]{2,1,0:T(8,128)(2,1)} %bitcast.16), custom_call_target="tpu_custom_call" | custom-call | flops 3489660928 | bytes 16777216 | tf_op jit(solution)/shard_map/pallas_call | solution.py:306
  92.8 41.2 %shard_map.70 = (bf16[208,1024]{1,0:T(8,128)(2,1)S(1)}, f32[208,208]{1,0:T(8,128)S(1)}) custom-call(bf16[208,1024]{1,0:T(8,128)(2,1)S(1)} %shard_map.69.refs_0_, bf16[2,1024,8192]{2,1,0:T(8,128)(2,1)} %bitcast.15, bf16[2,2,4,208,208]{4,3,2,1,0:T(8,128)(2,1)S(1)} %pad_add_fusion.refs_2_, f32[1,1024]{1,0:T(1,128)S(1)} %bitcast.12), custom_call_target="tpu_custom_call" | custom-call | flops 3489660928 | bytes 16777216 | tf_op jit(solution)/shard_map/pallas_call | solution.py:306
  134.0 0.8 multiply_bitcast_fusion
  134.8 0.0 all-reduce.7.cloned.1.call-update
  134.8 36.9 %shard_map.71 = bf16[208,1024]{1,0:T(8,128)(2,1)S(1)} custom-call(bf16[208,1024]{1,0:T(8,128)(2,1)S(1)} %get-tuple-element.7.refs_0_, bf16[2,1024,8192]{2,1,0:T(8,128)(2,1)} %bitcast.17), custom_call_target="tpu_custom_call" | custom-call | flops 3489660928 | bytes 16777216 | tf_op jit(solution)/shard_map/pallas_call | solution.py:306
  171.8 0.8 slice.19
  172.5 87.4 %all-reduce.7.cloned.1.call-done = (f32[1,198,198]{2,1,0:T(8,128)}, f32[1,198,198]{2,1,0:T(8,128)}) async-done(((f32[1,198,198]{2,1,0:T(8,128)}, f32[1,198,198]{2,1,0:T(8,128)}), (f32[1,198,198]{2,1,0:T(8,128)}, f32[1,198,198]{2,1,0:T(8,128)})) %all-reduce.7.cloned.1.call-update) | async-done | bytes 313648 | tf_op jit(solution)/shard_map/psum | solution.py:375
  259.9 1.1 pad_maximum_fusion
  261.0 1.0 copy.9
  (2 shorter events, 0.0 us)
Async XLA Ops:
  7.2 4.0 %copy-start.1 = (bf16[2,4,66,264]{3,1,2,0:T(4,128)(2,1)S(1)}, bf16[2,4,66,264]{3,1,2,0:T(4,128)(2,1)}, u32[]{:S(2)}) copy-start(bf16[2,4,66,264]{3,1,2,0:T(4,128)(2,1)} %param.7) | copy-start | bytes 836356
  7.2 252.8 %all-reduce.7.cloned.1.call-start = ((), (), s32[]{:S(2)}) async-start(), calls=%async_computation | async-start | bytes 819200 | tf_op jit(solution)/shard_map/psum | solution.py:375
  8.6 3.8 %copy-start = (bf16[198,1024]{1,0:T(8,128)(2,1)S(1)}, bf16[198,1024]{1,0:T(8,128)(2,1)}, u32[]{:S(2)}) copy-start(bf16[198,1024]{1,0:T(8,128)(2,1)} %param.5) | copy-start | bytes 1216516
Sparse Core Ops, SparseCore 0:
  135.0 124.9 all-reduce.6

commit v2 on v1

--- a/solution.py
+++ b/solution.py
@@ -46,8 +46,9 @@
          wbuf, psend, own, prec, xrec, cg, zsend, zrec,
          wsem, pss, prs, xss, xrs, zss, zrs) = refs
     else:
-        (state, weight, out,
+        (state, weight, gram, out, gram_out,
          wbuf, psend, own, prec, xrec, zown, zin, zsum, zrec,
+         gsend, grec, gss, grs,
          wsem, pss, prs, xss, xrs, zss, zrs) = refs
     chips = 1 << bits
     depth = state.shape[1]
@@ -144,6 +145,7 @@
                 parts.append(total[0])
         return parts
 
+    scale = 1.0 / weight.shape[2]
     columns = [pl.ds(c * width, width) for c in range(chunks)]
 
     if mixing:
@@ -257,16 +259,58 @@
                 z_back_copy(c).wait_recv()
                 out[:, columns[c]] = zin[c]
 
+        def gram_copy(i):
+            bond, mpo = j, z
+            if i == 0:
+                bond = 2 * me + 1 - core
+            elif i <= bits:
+                bond = 2 * flip(me, i - 1) + core
+            else:
+                mpo = jnp.where(is_mid, across if i == bits + 2 else outer, inner)
+            return remote(gsend.at[i], grec.at[i], gss.at[i], grs.at[i], bond, mpo)
+
+        def gram_sum(i):
+            return gsend[i].astype(F32) + grec[i].astype(F32)
+
+        def gram_step(t):
+            if t <= bits + 1:
+                if t == 0:
+                    gsend[t] = gram[...].astype(BF16)
+                else:
+                    gram_copy(t - 1).wait_recv()
+                    gsend[t] = gram_sum(t - 1).astype(BF16)
+                if t <= bits:
+                    gram_copy(t).start()
+                else:
+                    @pl.when(is_end)
+                    def _():
+                        gram_copy(t).start()
+            elif t <= bits + 3:
+                @pl.when(is_mid)
+                def _():
+                    gram_copy(t - 1).wait_recv()
+                    gsend[t] = gram_sum(t - 1).astype(BF16)
+                    gram_copy(t).start()
+                    if t == bits + 3:
+                        gram_out[...] = gsend[t].astype(F32) * scale
+            elif t == bits + 4:
+                @pl.when(is_end)
+                def _():
+                    gram_copy(t - 1).wait_recv()
+                    gram_out[...] = grec[t - 1].astype(F32) * scale
+
         end_sends, mid_sends = (z_end_copy,), (z_mid_copy, z_back_copy)
 
     stages = [multiply, pair_sum]
     for step in range(bits - 1):
         stages.append(functools.partial(xy_sum, step=step))
     stages += [lambda c: z_first(c, xy_sum(c, bits - 1)), z_second, z_third, z_fourth]
-    for t in range(chunks + len(stages) - 1):
+    for t in range(max(chunks + len(stages) - 1, bits + 5)):
         for number, stage in enumerate(stages):
             if 0 <= t - number < chunks:
                 stage(t - number)
+        if not mixing:
+            gram_step(t)
 
     for c in range(chunks):
         pair_copy(c).wait_send()
@@ -278,11 +322,20 @@
         def _():
             for copy in end_sends:
                 copy(c).wait_send()
+            if not mixing and c == 0:
+                gram_copy(bits + 1).wait_send()
 
         @pl.when(is_mid)
         def _():
             for copy in mid_sends:
                 copy(c).wait_send()
+            if not mixing and c == 0:
+                for i in (bits + 2, bits + 3):
+                    gram_copy(i).wait_send()
+
+    if not mixing:
+        for i in range(bits + 1):
+            gram_copy(i).wait_send()
 
 
 def apply_site(bits, site, mixing, state, weight, *extra):
@@ -296,12 +349,13 @@
     parts = pltpu.VMEM((chunks, 2, chips, rows, half), BF16)
     piece = pltpu.VMEM((chunks, rows, width), BF16)
     out_shape = [jax.ShapeDtypeStruct((rows, block), BF16)]
+    out_shape.append(jax.ShapeDtypeStruct((rows, rows), F32))
+    dma = pltpu.SemaphoreType.DMA
     if mixing:
-        out_shape.append(jax.ShapeDtypeStruct((rows, rows), F32))
         z_scratch = [pltpu.VMEM((chunks, 4, rows, width), BF16), piece, piece]
     else:
-        z_scratch = [piece] * 4
-    dma = pltpu.SemaphoreType.DMA
+        gram_parts = pltpu.VMEM((bits + 4, rows, rows), BF16)
+        z_scratch = [piece] * 4 + [gram_parts] * 2 + [dma((bits + 4,))] * 2
     z_copies = 4 if mixing else 3
     return pl.pallas_call(
         functools.partial(site_kernel, bits, chunks, site, mixing),
@@ -371,9 +425,8 @@
         grams = []
         for site in range(SITE_COUNT):
             kept, gram = apply_site(bits, site, True, state, sites, ops, mask[site])
-            gram = gram[:row_count, :row_count] / (block * mesh.shape["bond"])
-            grams.append(lax.psum(gram, ("bond", "mpo")))
-            (state,) = apply_site(bits, site, False, kept, turns)
+            state, gram = apply_site(bits, site, False, kept, turns, gram)
+            grams.append(gram[:row_count, :row_count])
         return state[:row_count], jnp.stack(grams)
 
     return jax.shard_map(

time: 269 us -> 172 us (0.64)
  waiting for transfers between devices: 87.4 us -> 0 us
  between operations: 14.1 us -> 0.75 us
  Pallas kernels: 158 us -> 164 us
    psum x1 -> x0, waiting for transfers between devices: 87.4 us -> none  [on_device(): grams.append(lax.psum(gram, ('bond', 'mpo')))]
    pallas_call x4, Pallas kernels: 158 us -> 164 us  [apply_site(): pl.pallas_call(functools.partial(site_kernel, bits, chunks, site, mixing)...]
  transfers between devices with their start and end apart: 1 -> 0, of which waited for: 1 -> 0; matrix products, arithmetic and copies ran while one was open for 0% -> 0% of each run, Pallas kernels for 14% -> 0%
where the time goes in v2:
time: 172 us
  Pallas kernels  164 us (95%)
  matrix products  2.55 us (1%)
  local copies, waits for them, and re-layouts  2.41 us (1%)
  other arithmetic  2.04 us (1%)
    pallas_call x4, Pallas kernels, apply_site(): pl.pallas_call(functools.partial(site_kernel, bits, chunks, site, mixing)...  164 us

profile of v2, /device:TPU:0, one launch (start us, length us, event | category | flops | bytes accessed | tf_op | source)
XLA Modules:
  0.0 171.9 jit_solution(928335395089411741)
XLA Ops:
  0.6 0.0 copy-start.1
  0.6 0.0 copy-start
  0.7 1.3 and_select_fusion.2
  2.0 0.1 and_select_fusion
  2.1 2.5 %fusion = f32[2,8,128]{2,1,0:T(8,128)S(1)} fusion(s32[2,8192]{1,0:T(2,128)S(1)} %and_select_fusion, s32[2,8192]{1,0:T(2,128)S(1)} %get-tuple-element.20), kind=kOutput, calls=%fused_computation.1 | convolution fusion | flops 35782656 | bytes 139264 | tf_op jit(solution)/shard_map/khi,khj->kij/dot_general | solution.py:409
  4.6 0.0 copy-done.1
  4.7 0.2 constant_dynamic-slice_fusion.1
  4.9 0.2 copy.7
  5.1 0.2 copy.8
  5.3 0.1 maximum_bitcast_fusion
  5.3 0.0 copy-done
  5.4 0.5 pad_add_fusion.refs_2_
  5.9 43.7 %shard_map.68 = (bf16[208,1024]{1,0:T(8,128)(2,1)S(1)}, f32[208,208]{1,0:T(8,128)S(1)}) custom-call(bf16[208,1024]{1,0:T(8,128)(2,1)S(1)} %pad.16.refs_0_, bf16[2,1024,8192]{2,1,0:T(8,128)(2,1)} %bitcast.14, bf16[2,2,4,208,208]{4,3,2,1,0:T(8,128)(2,1)S(1)} %pad_add_fusion.refs_2_, f32[1,1024]{1,0:T(1,128)S(1)} %bitcast.13), custom_call_target="tpu_custom_call" | custom-call | flops 3489660928 | bytes 16777216 | tf_op jit(solution)/shard_map/pallas_call | solution.py:360
  49.6 39.7 %shard_map.69 = (bf16[208,1024]{1,0:T(8,128)(2,1)S(1)}, f32[208,208]{1,0:T(8,128)S(1)}) custom-call(bf16[208,1024]{1,0:T(8,128)(2,1)S(1)} %get-tuple-element.10.refs_0_, bf16[2,1024,8192]{2,1,0:T(8,128)(2,1)} %bitcast.16, f32[208,208]{1,0:T(8,128)S(1)} %get-tuple-element.11.refs_2_), custom_call_target="tpu_custom_call" | custom-call | flops 3489660928 | bytes 16777216 | tf_op jit(solution)/shard_map/pallas_call | solution.py:360
  89.3 41.2 %shard_map.70 = (bf16[208,1024]{1,0:T(8,128)(2,1)S(1)}, f32[208,208]{1,0:T(8,128)S(1)}) custom-call(bf16[208,1024]{1,0:T(8,128)(2,1)S(1)} %get-tuple-element.12.refs_0_, bf16[2,1024,8192]{2,1,0:T(8,128)(2,1)} %bitcast.15, bf16[2,2,4,208,208]{4,3,2,1,0:T(8,128)(2,1)S(1)} %pad_add_fusion.refs_2_, f32[1,1024]{1,0:T(1,128)S(1)} %bitcast.12), custom_call_target="tpu_custom_call" | custom-call | flops 3489660928 | bytes 16777216 | tf_op jit(solution)/shard_map/pallas_call | solution.py:360
  130.5 39.6 %shard_map.71 = (bf16[208,1024]{1,0:T(8,128)(2,1)S(1)}, f32[208,208]{1,0:T(8,128)S(1)}) custom-call(bf16[208,1024]{1,0:T(8,128)(2,1)S(1)} %get-tuple-element.13.refs_0_, bf16[2,1024,8192]{2,1,0:T(8,128)(2,1)} %bitcast.17, f32[208,208]{1,0:T(8,128)S(1)} %get-tuple-element.14.refs_2_), custom_call_target="tpu_custom_call" | custom-call | flops 3489660928 | bytes 16777216 | tf_op jit(solution)/shard_map/pallas_call | solution.py:360
  170.1 0.8 slice.19
  170.9 1.0 copy.9
  (4 shorter events, 0.1 us)
Async XLA Ops:
  0.6 4.0 %copy-start.1 = (bf16[2,4,66,264]{3,1,2,0:T(4,128)(2,1)S(1)}, bf16[2,4,66,264]{3,1,2,0:T(4,128)(2,1)}, u32[]{:S(2)}) copy-start(bf16[2,4,66,264]{3,1,2,0:T(4,128)(2,1)} %param.7) | copy-start | bytes 836356
  0.6 4.7 %copy-start = (bf16[198,1024]{1,0:T(8,128)(2,1)S(1)}, bf16[198,1024]{1,0:T(8,128)(2,1)}, u32[]{:S(2)}) copy-start(bf16[198,1024]{1,0:T(8,128)(2,1)} %param.5) | copy-start | bytes 1216516

commit v3 on v2

--- a/solution.py
+++ b/solution.py
@@ -11,6 +11,7 @@
 SITE_COUNT = 2
 MESH = pl.DeviceIdType.MESH
 F32 = jnp.float32
+A_SCRATCH = 15
 BF16 = jnp.bfloat16
 
 
@@ -40,7 +41,7 @@
     return z, is_mid, inner, outer, 3 - z
 
 
-def site_kernel(bits, chunks, site, mixing, *refs):
+def phase(bits, chunks, site, mixing, refs):
     if mixing:
         (state, weight, ops, mask, out, gram,
          wbuf, psend, own, prec, xrec, cg, zsend, zrec,
@@ -75,25 +76,7 @@
             def _(r):
                 weight_copy(c, other, r).start()
 
-    barrier = pltpu.get_barrier_semaphore()
-
-    def greet(bond, mpo):
-        pl.semaphore_signal(barrier, inc=1, device_id=(bond, mpo), device_id_type=MESH)
-
-    greet(2 * me + 1 - core, z)
-    for b in range(bits):
-        greet(2 * flip(me, b) + core, z)
-
-    @pl.when(is_mid)
-    def _():
-        greet(j, outer)
-        greet(j, across)
-        pl.semaphore_wait(barrier, bits + 3)
-
-    @pl.when(is_end)
-    def _():
-        greet(j, inner)
-        pl.semaphore_wait(barrier, bits + 2)
+    yield
 
     def remote(src, dst, ss, rs, bond, mpo):
         return pltpu.make_async_remote_copy(
@@ -312,6 +295,8 @@
         if not mixing:
             gram_step(t)
 
+    yield
+
     for c in range(chunks):
         pair_copy(c).wait_send()
         for step in range(bits):
@@ -338,50 +323,95 @@
             gram_copy(i).wait_send()
 
 
-def apply_site(bits, site, mixing, state, weight, *extra):
+def greet_peers(bits):
+    j = lax.axis_index("bond")
+    me, core = j // 2, j % 2
+    z, is_mid, inner, outer, across = z_roles()
+    is_end = jnp.logical_not(is_mid)
+    barrier = pltpu.get_barrier_semaphore()
+
+    def greet(bond, mpo):
+        pl.semaphore_signal(barrier, inc=1, device_id=(bond, mpo), device_id_type=MESH)
+
+    greet(2 * me + 1 - core, z)
+    for b in range(bits):
+        greet(2 * flip(me, b) + core, z)
+
+    @pl.when(is_mid)
+    def _():
+        greet(j, outer)
+        greet(j, across)
+        pl.semaphore_wait(barrier, bits + 3)
+
+    @pl.when(is_end)
+    def _():
+        greet(j, inner)
+        pl.semaphore_wait(barrier, bits + 2)
+
+
+def site_kernel(bits, chunks, site, *refs):
+    state, tensor, turn, ops, mask, out, gram_out, kept, gram = refs[:9]
+    first, second = refs[9:9 + A_SCRATCH], refs[9 + A_SCRATCH:]
+    phases = [
+        phase(bits, chunks, site, True, (state, tensor, ops, mask, kept, gram, *first)),
+        phase(bits, chunks, site, False, (kept, turn, gram, out, gram_out, *second)),
+    ]
+    for part in phases:
+        next(part)
+    greet_peers(bits)
+    for part in phases:
+        next(part)
+    for part in phases:
+        next(part, None)
+
+
+def apply_site(bits, site, state, tensor, turn, ops, mask):
     rows, depth = state.shape
     chips = 1 << bits
-    block = weight.shape[2] // (2 * chips)
+    block = tensor.shape[2] // (2 * chips)
     chunks = max(1, block // 256)
     width = block // chunks
-    half = width // 2
+    dma = pltpu.SemaphoreType.DMA
     vmem = pl.BlockSpec(memory_space=pltpu.VMEM)
-    parts = pltpu.VMEM((chunks, 2, chips, rows, half), BF16)
+    hbm = pl.BlockSpec(memory_space=pl.ANY)
+    parts = pltpu.VMEM((chunks, 2, chips, rows, width // 2), BF16)
     piece = pltpu.VMEM((chunks, rows, width), BF16)
-    out_shape = [jax.ShapeDtypeStruct((rows, block), BF16)]
-    out_shape.append(jax.ShapeDtypeStruct((rows, rows), F32))
-    dma = pltpu.SemaphoreType.DMA
-    if mixing:
-        z_scratch = [pltpu.VMEM((chunks, 4, rows, width), BF16), piece, piece]
-    else:
-        gram_parts = pltpu.VMEM((bits + 4, rows, rows), BF16)
-        z_scratch = [piece] * 4 + [gram_parts] * 2 + [dma((bits + 4,))] * 2
-    z_copies = 4 if mixing else 3
-    return pl.pallas_call(
-        functools.partial(site_kernel, bits, chunks, site, mixing),
-        out_shape=out_shape,
-        in_specs=[vmem, pl.BlockSpec(memory_space=pl.ANY)] + [vmem] * len(extra),
-        out_specs=[vmem] * len(out_shape),
-        scratch_shapes=[
-            pltpu.VMEM((2 * chips * chunks, depth, width), BF16),
-            parts, parts, parts, parts,
-            *z_scratch,
+    gram_parts = pltpu.VMEM((bits + 4, rows, rows), BF16)
+    common = [pltpu.VMEM((2 * chips * chunks, depth, width), BF16)] + [parts] * 4
+
+    def semaphores(z_copies):
+        return [
             dma((2 * chips * chunks,)),
             dma((chunks,)), dma((chunks,)),
             dma((chunks, bits, 2)), dma((chunks, bits, 2)),
             dma((chunks, z_copies)), dma((chunks, z_copies)),
+        ]
+
+    first = common + [pltpu.VMEM((chunks, 4, rows, width), BF16), piece, piece] + semaphores(4)
+    second = (common + [piece] * 4 + [gram_parts] * 2 + [dma((bits + 4,))] * 2
+              + semaphores(3))
+    return pl.pallas_call(
+        functools.partial(site_kernel, bits, chunks, site),
+        out_shape=[
+            jax.ShapeDtypeStruct((rows, block), BF16),
+            jax.ShapeDtypeStruct((rows, rows), F32),
+        ],
+        in_specs=[vmem, hbm, hbm, vmem, vmem],
+        out_specs=[vmem] * 2,
+        scratch_shapes=[
+            pltpu.VMEM((rows, block), BF16), pltpu.VMEM((rows, rows), F32), *first, *second,
         ],
         compiler_params=pltpu.CompilerParams(
-            collective_id=2 * site + (0 if mixing else 1),
+            collective_id=site,
             has_side_effects=True,
-            vmem_limit_bytes=48 * 1024 * 1024,
+            vmem_limit_bytes=60 * 1024 * 1024,
         ),
         cost_estimate=pl.CostEstimate(
-            flops=2 * rows * depth * weight.shape[2],
-            bytes_accessed=2 * depth * weight.shape[2],
+            flops=4 * rows * depth * tensor.shape[2],
+            bytes_accessed=4 * depth * tensor.shape[2],
             transcendentals=0,
         ),
-    )(state, weight, *extra)
+    )(state, tensor, turn, ops, mask)
 
 
 def operator_blocks(operator_tensors, rows):
@@ -424,8 +454,7 @@
         state = jnp.pad(carried, ((0, rows - row_count), (0, 0)))
         grams = []
         for site in range(SITE_COUNT):
-            kept, gram = apply_site(bits, site, True, state, sites, ops, mask[site])
-            state, gram = apply_site(bits, site, False, kept, turns, gram)
+            state, gram = apply_site(bits, site, state, sites, turns, ops, mask[site])
             grams.append(gram[:row_count, :row_count])
         return state[:row_count], jnp.stack(grams)
 

time: 172 us -> 177 us (1.029)
  local copies, waits for them, and re-layouts: 2.41 us -> 5.7 us
    pallas_call x4 -> x2, Pallas kernels: 164 us -> 165 us  [apply_site(): pl.pallas_call(functools.partial(site_kernel, bits, chunks, site), out_sh...]
where the time goes in v3:
time: 177 us
  Pallas kernels  165 us (93%)
  local copies, waits for them, and re-layouts  5.7 us (3%)
  other arithmetic  3.27 us (2%)
  matrix products  2.55 us (1%)
    pallas_call x2, Pallas kernels, apply_site(): pl.pallas_call(functools.partial(site_kernel, bits, chunks, site), out_sh...  165 us

profile of v3, /device:TPU:0, one launch (start us, length us, event | category | flops | bytes accessed | tf_op | source)
XLA Modules:
  0.0 177.0 jit_solution(15147177292555315269)
XLA Ops:
  0.6 0.0 copy-start.2
  0.6 0.0 copy-start
  0.7 1.3 and_select_fusion.2
  2.0 0.1 and_select_fusion
  2.1 2.5 %fusion = f32[2,8,128]{2,1,0:T(8,128)S(1)} fusion(s32[2,8192]{1,0:T(2,128)S(1)} %and_select_fusion, s32[2,8192]{1,0:T(2,128)S(1)} %get-tuple-element.12), kind=kOutput, calls=%fused_computation.1 | convolution fusion | flops 35782656 | bytes 139264 | tf_op jit(solution)/shard_map/khi,khj->kij/dot_general | solution.py:439
  4.6 0.6 fusion.5
  5.3 0.0 copy-done.2
  5.3 0.2 constant_dynamic-slice_fusion.1
  5.5 0.2 copy.7
  5.7 0.2 copy.8
  5.9 0.1 maximum_bitcast_fusion
  5.9 0.0 copy-done
  5.9 0.8 pad.16.refs_0_
  6.7 1.7 pad_add_fusion.refs_3_
  8.5 83.9 %shard_map.68 = (bf16[208,1024]{1,0:T(8,128)(2,1)}, f32[208,208]{1,0:T(8,128)}) custom-call(bf16[208,1024]{1,0:T(8,128)(2,1)} %pad.16.refs_0_, bf16[2,1024,8192]{2,1,0:T(8,128)(2,1)} %bitcast.12, bf16[2,1024,8192]{2,1,0:T(8,128)(2,1)} %bitcast.14, bf16[2,2,4,208,208]{4,3,2,1,0:T(8,128)(2,1)} %pad_add_fusion.refs_3_, f32[1,1024]{1,0:T(1,128)} %bitcast.19), custom_call_target="tpu_custom_call" | custom-call | flops 6979321856 | bytes 33554432 | tf_op jit(solution)/shard_map/pallas_call | solution.py:393
  92.4 0.0 copy-start.1
  92.4 80.8 %shard_map.69 = (bf16[208,1024]{1,0:T(8,128)(2,1)}, f32[208,208]{1,0:T(8,128)}) custom-call(bf16[208,1024]{1,0:T(8,128)(2,1)} %get-tuple-element.6.refs_0_, bf16[2,1024,8192]{2,1,0:T(8,128)(2,1)} %bitcast.13, bf16[2,1024,8192]{2,1,0:T(8,128)(2,1)} %bitcast.15, bf16[2,2,4,208,208]{4,3,2,1,0:T(8,128)(2,1)} %pad_add_fusion.refs_3_, f32[1,1024]{1,0:T(1,128)} %bitcast.18), custom_call_target="tpu_custom_call" | custom-call | flops 6979321856 | bytes 33554432 | tf_op jit(solution)/shard_map/pallas_call | solution.py:393
  173.2 1.8 %slice.19 = bf16[198,1024]{1,0:T(8,128)(2,1)} slice(bf16[208,1024]{1,0:T(8,128)(2,1)} %get-tuple-element.7), slice={[0:198], [0:1024]} | slice | bytes 811008 | tf_op jit(solution)/shard_map/slice | solution.py:459
  175.0 0.0 copy-done.1
  175.0 1.0 slice_bitcast_fusion
  176.0 1.0 copy.9
  (1 shorter events, 0.0 us)
Async XLA Ops:
  0.6 4.6 %copy-start.2 = (bf16[2,4,66,264]{3,1,2,0:T(4,128)(2,1)S(1)}, bf16[2,4,66,264]{3,1,2,0:T(4,128)(2,1)}, u32[]{:S(2)}) copy-start(bf16[2,4,66,264]{3,1,2,0:T(4,128)(2,1)} %param.7) | copy-start | bytes 836356
  0.6 5.3 %copy-start = (bf16[198,1024]{1,0:T(8,128)(2,1)S(1)}, bf16[198,1024]{1,0:T(8,128)(2,1)}, u32[]{:S(2)}) copy-start(bf16[198,1024]{1,0:T(8,128)(2,1)} %param.5) | copy-start | bytes 1216516
  92.4 82.6 %copy-start.1 = (f32[208,208]{1,0:T(8,128)S(1)}, f32[208,208]{1,0:T(8,128)}, u32[]{:S(2)}) copy-start(f32[208,208]{1,0:T(8,128)} %get-tuple-element.8) | copy-start | bytes 519172
